TPU v7x, 256 devices: a whole 4x4x8 slice. The times are simulated.
256 devices in a mesh: link: 32 (over z, x), intv: 8 (over y, core).
Axes of the slice: x: 4, y: 4, z: 8, core: 2. Of those that a mesh axis runs over, the one named last changes fastest.
Arguments:
- slab: bfloat16 [256, 16, 262144], P('intv', None, 'link'), may hold values from -6 to 6
- interval_factor: float32 [256, 64], P('intv'), may hold values from -6 to 6
- day_factor: float32 [16, 64], replicated, may hold values from -6 to 6
Outputs:
- link_new: float32 [262144, 64], P(('link', 'intv'))
- interval_new: float32 [256, 64], P('intv')
- day_new: float32 [16, 64], replicated
All inputs are finite; a program needn't handle non-finite values.
Results may differ from a plain program's by a relative error of at most 0.0024.
The roundings to bfloat16 on the way count: a program that leaves them out, or rounds other values in their place, can miss the bound.
Values may be sent and summed in bfloat16 or wider, within the bound.
No kernel may reach another device: no remote copies, remote signals or barrier semaphores. Data moves between devices by JAX's collectives and lax.ppermute only.
A program may use at most 64 MiB of HBM per device.

v0:
```python
import jax
import jax.numpy as jnp
from jax import lax
from jax.sharding import PartitionSpec as P


def solve_rows(system, rhs):
    rank = system.shape[0]
    shifted = system + 0.01 * jnp.trace(system) / rank * jnp.eye(rank, dtype=system.dtype)
    factor = jnp.linalg.cholesky(shifted)
    return jax.scipy.linalg.cho_solve((factor, True), rhs.T).T


def gram_of(matrix):
    return jnp.dot(matrix.T, matrix, precision=lax.Precision.HIGHEST)


def body(slab, interval_factor, day_factor):
    intervals, days, links = slab.shape
    rank = day_factor.shape[1]
    flat = slab.reshape(intervals * days, links)
    gram_day = gram_of(day_factor)
    gram_interval = lax.psum(gram_of(interval_factor), "intv")
    khatri = (
        (interval_factor[:, None, :] * day_factor[None, :, :])
        .reshape(intervals * days, rank)
        .astype(jnp.bfloat16)
    )
    system_link = gram_interval * gram_day
    owned_sums = lax.psum_scatter(
        lax.dot_general(flat, khatri, (((0,), (0,)), ((), ())), preferred_element_type=jnp.float32),
        "intv",
        scatter_dimension=0,
        tiled=True,
    )
    link_new = solve_rows(system_link, owned_sums)
    gram_link = lax.psum(gram_of(link_new), ("link", "intv"))
    link_block = lax.all_gather(link_new.astype(jnp.bfloat16), "intv", axis=0, tiled=True)
    partial_sums = jnp.dot(flat, link_block, preferred_element_type=jnp.float32).reshape(
        intervals, days, rank
    )
    interval_part = jnp.sum(partial_sums * day_factor[None, :, :], axis=1)
    interval_sums = lax.psum(interval_part, "link")
    interval_new = solve_rows(gram_link * gram_day, interval_sums)
    gram_new = lax.psum(gram_of(interval_new), "intv")
    day_part = jnp.sum(partial_sums * interval_new[:, None, :], axis=0)
    day_sums = lax.psum(day_part, ("link", "intv"))
    day_new = solve_rows(gram_link * gram_new, day_sums)
    return (link_new, interval_new, day_new)


def solution(mesh):
    placed = (P("intv", None, "link"), P("intv", None), P())
    return jax.shard_map(
        body,
        mesh=mesh,
        in_specs=placed,
        out_specs=(P(("link", "intv"), None), P("intv", None), P()),
        check_vma=False,
    )
```

profile of v0, /device:TPU:32, one launch (start us, length us, event | category | flops | bytes accessed | tf_op | source)
XLA Modules:
  0.0 413.3 jit_solution(11994552276993962413)
XLA Ops:
  7.2 0.0 copy-start.3
  7.2 0.0 copy-start.1
  7.2 0.0 reduce-scatter.2.cloned.1.call-start
  7.2 6.4 %convolution_bitcast_fusion = f32[8192,64]{0,1:T(8,128)} fusion(bf16[32,16,8192]{2,1,0:T(8,128)(2,1)} %param.4, f32[16,64]{1,0:T(8,128)} %param.6, f32[32,64]{1,0:T(8,128)} %param.5), kind=kOutput, calls=%fused_computation | convolution fusion | flops 536936448 | bytes 10498048 | tf_op jit(solution)/shard_map/dot_general | solution.py:31
  13.6 0.0 reduce-scatter.2.cloned.1.call-update
  13.6 0.0 all-gather.2.cloned.1.call-start
  13.7 0.0 copy-done.1
  13.7 0.2 fusion.32
  13.9 25.9 %psum.35 = f32[64,64]{1,0:T(8,128)S(1)} all-reduce(f32[64,64]{1,0:T(8,128)S(1)} %fusion.32), channel_id=1, replica_groups=mesh['link'=32,'intv'=8] {'intv'}, use_global_device_ids=true, to_apply=%region_0.0 | all-reduce | flops 4096 | bytes 32768 | tf_op jit(solution)/shard_map/psum | solution.py:23
  39.8 0.0 copy-done.3
  39.8 0.8 fusion.26
  41.3 0.1 copy.15
  41.4 0.1 copy.16
  41.5 5.9 %cholesky.59 = f32[64,64]{1,0:T(8,128)S(1)} custom-call(f32[64,64]{1,0:T(8,128)S(1)} %copy.16), custom_call_target="Cholesky" | custom-call | tf_op jit(solution)/shard_map/jit(cholesky)/cholesky | solution.py:10
  47.4 0.6 compare_reduce_fusion.2
  48.1 0.7 fusion.2
  48.7 4.9 %custom-call.23 = f32[1,64,64]{1,2,0:T(8,128)S(1)} custom-call(f32[1,64,64]{2,1,0:T(8,128)S(1)} %fusion.2), custom_call_target="InvertDiagBlocksLowerTriangular" | custom-call | tf_op jit(solution)/shard_map/jit(_cho_solve)/triangular_solve | solution.py:11
  53.6 0.0 reduce-scatter.2.cloned.1.call-done
  53.6 1.4 fusion.17
  55.0 0.4 fusion.15
  55.4 0.0 copy-start
  55.4 0.7 bitcast_convert_fusion
  56.1 0.0 all-gather.2.cloned.1.call-update
  56.2 0.4 fusion.33
  56.5 78.2 %psum.36 = f32[64,64]{1,0:T(8,128)S(1)} all-reduce(f32[64,64]{1,0:T(8,128)S(1)} %fusion.33), channel_id=1, replica_groups=mesh['link'=32,'intv'=8] {'link','intv'}, use_global_device_ids=true, to_apply=%region_5.7 | all-reduce | flops 4096 | bytes 32768 | tf_op jit(solution)/shard_map/psum | solution.py:37
  134.8 0.6 fusion.28
  136.0 0.1 copy.17
  136.1 0.1 copy.18
  136.2 5.9 %cholesky.70 = f32[64,64]{1,0:T(8,128)S(1)} custom-call(f32[64,64]{1,0:T(8,128)S(1)} %copy.18), custom_call_target="Cholesky" | custom-call | tf_op jit(solution)/shard_map/jit(cholesky)/cholesky | solution.py:10
  142.1 0.6 compare_reduce_fusion.1
  142.7 0.7 fusion.3
  143.4 4.9 %custom-call.24 = f32[1,64,64]{1,2,0:T(8,128)S(1)} custom-call(f32[1,64,64]{2,1,0:T(8,128)S(1)} %fusion.3), custom_call_target="InvertDiagBlocksLowerTriangular" | custom-call | tf_op jit(solution)/shard_map/jit(_cho_solve)/triangular_solve | solution.py:11
  148.3 0.0 all-gather.2.cloned.1.call-done
  148.3 6.4 %convolution_bitcast_fusion.1 = f32[512,64]{0,1:T(8,128)S(1)} fusion(bf16[8192,64]{0,1:T(8,128)(2,1)} %all-gather.2.cloned.1.call-done, bf16[512,8192]{1,0:T(8,128)(2,1)} %bitcast.62), kind=kOutput, calls=%fused_computation.1 | convolution fusion | flops 536870912 | bytes 9568256 | tf_op jit(solution)/shard_map/dot_general | solution.py:39
  154.7 0.1 copy.19
  154.9 0.1 multiply_reduce_fusion.1
  154.9 132.4 %psum.37 = f32[32,64]{1,0:T(8,128)S(1)} all-reduce(f32[32,64]{1,0:T(8,128)S(1)} %multiply_reduce_fusion.1), channel_id=1, replica_groups=mesh['link'=32,'intv'=8] {'link'}, use_global_device_ids=true, to_apply=%region_8.10 | all-reduce | flops 2048 | bytes 16384 | tf_op jit(solution)/shard_map/psum | solution.py:43
  287.3 0.2 fusion.12
  287.6 0.2 fusion.10
  287.8 0.0 copy-start.2
  287.8 0.2 fusion.34
  288.1 80.1 %psum.39 = f32[16,64]{1,0:T(8,128)S(1)} all-reduce(f32[16,64]{1,0:T(8,128)S(1)} %multiply_reduce_fusion), channel_id=1, replica_groups=mesh['link'=32,'intv'=8] {'link','intv'}, use_global_device_ids=true, to_apply=%region_12.14 | all-reduce | flops 1024 | bytes 8192 | tf_op jit(solution)/shard_map/psum | solution.py:47
  368.2 23.6 %psum.38 = f32[64,64]{1,0:T(8,128)S(1)} all-reduce(f32[64,64]{1,0:T(8,128)S(1)} %fusion.34), channel_id=1, replica_groups=mesh['link'=32,'intv'=8] {'intv'}, use_global_device_ids=true, to_apply=%region_9.11 | all-reduce | flops 4096 | bytes 32768 | tf_op jit(solution)/shard_map/psum | solution.py:45
  391.8 0.6 fusion.30
  393.1 0.1 copy.20
  393.2 0.1 copy.21
  393.3 5.9 %cholesky.81 = f32[64,64]{1,0:T(8,128)S(1)} custom-call(f32[64,64]{1,0:T(8,128)S(1)} %copy.21), custom_call_target="Cholesky" | custom-call | tf_op jit(solution)/shard_map/jit(cholesky)/cholesky | solution.py:10
  399.2 0.6 compare_reduce_fusion
  399.8 0.7 fusion.4
  400.5 4.9 %custom-call.25 = f32[1,64,64]{1,2,0:T(8,128)S(1)} custom-call(f32[1,64,64]{2,1,0:T(8,128)S(1)} %fusion.4), custom_call_target="InvertDiagBlocksLowerTriangular" | custom-call | tf_op jit(solution)/shard_map/jit(_cho_solve)/triangular_solve | solution.py:11
  405.4 0.3 fusion.7
  405.6 0.8 fusion.5
  406.5 0.0 copy-done
  406.5 0.0 copy-done.2
  (10 shorter events, 0.2 us)
Async XLA Ops:
  7.2 32.7 %copy-start.3 = (f32[16,64]{1,0:T(8,128)S(1)}, f32[16,64]{1,0:T(8,128)}, u32[]{:S(2)}) copy-start(f32[16,64]{1,0:T(8,128)} %param.6) | copy-start | bytes 12292
  7.2 6.5 %copy-start.1 = (f32[32,64]{1,0:T(8,128)S(1)}, f32[32,64]{1,0:T(8,128)}, u32[]{:S(2)}) copy-start(f32[32,64]{1,0:T(8,128)} %param.5) | copy-start | bytes 24580
  7.2 46.4 %reduce-scatter.2.cloned.1.call-start = ((), (), s32[]{:S(2)}) async-start(), calls=%async_computation.1 | async-start | bytes 2359296 | tf_op jit(solution)/shard_map/reduce_scatter | solution.py:30
  13.6 134.7 %all-gather.2.cloned.1.call-start = ((), (), s32[]{:S(2)}) async-start(), calls=%async_computation.2 | async-start | bytes 1179648 | tf_op jit(solution)/shard_map/all_gather | solution.py:38
  55.4 351.1 %copy-start = (f32[64,1024]{1,0:T(8,128)}, f32[64,1024]{1,0:T(8,128)S(1)}, u32[]{:S(2)}) copy-start(f32[64,1024]{1,0:T(8,128)S(1)} %fusion.15) | copy-start | bytes 786436
  287.8 118.7 %copy-start.2 = (f32[64,32]{0,1:T(8,128)}, f32[64,32]{0,1:T(8,128)S(1)}, u32[]{:S(2)}) copy-start(f32[64,32]{0,1:T(8,128)S(1)} %fusion.10) | copy-start | bytes 24580
Sparse Core Ops, SparseCore 0:
  13.8 38.8 reduce-scatter.1
  56.3 25.8 all-gather.1
where the time goes:
time: 414 us; the launch traced here: 413 us
  blocking collectives  340 us (82%)
  other arithmetic  38.4 us (9%)
  matrix products  17.7 us (4%)
  between operations  16.2 us (4%)
    psum x1, blocking collectives, body(): interval_sums = lax.psum(interval_part, 'link')  132 us
    psum x1, blocking collectives, body(): day_sums = lax.psum(day_part, ('link', 'intv'))  80.1 us
    psum x1, blocking collectives, body(): gram_link = lax.psum(gram_of(link_new), ('link', 'intv'))  78.2 us
    psum x1, blocking collectives, body(): gram_interval = lax.psum(gram_of(interval_factor), 'intv')  25.9 us
    psum x1, blocking collectives, body(): gram_new = lax.psum(gram_of(interval_new), 'intv')  23.6 us
    another operation x9, other arithmetic, solve_rows(): factor = jnp.linalg.cholesky(shifted)  19.6 us
    another operation x6, other arithmetic, solve_rows(): return jax.scipy.linalg.cho_solve((factor, True), rhs.T).T  16.6 us
  transfers between devices with their start and end apart: 2, of which 0 were waited for; matrix products, arithmetic and copies ran while one was open for 6% of the time, Pallas kernels for 0%

commit v1 on v0

--- a/solution.py
+++ b/solution.py
@@ -40,7 +40,21 @@
         intervals, days, rank
     )
     interval_part = jnp.sum(partial_sums * day_factor[None, :, :], axis=1)
-    interval_sums = lax.psum(interval_part, "link")
+
+    def assign_target(field_in):
+        num_devices = lax.axis_size("link")
+
+        def press_threads(w1, y2):
+            if y2 >= num_devices:
+                return w1
+            blocks_here = []
+            for num in range(num_devices):
+                blocks_here.append((num, num ^ y2))
+            return press_threads(w1 + lax.ppermute(w1, "link", blocks_here), 2 * y2)
+
+        return press_threads(field_in, 1)
+
+    interval_sums = assign_target(interval_part)
     interval_new = solve_rows(gram_link * gram_day, interval_sums)
     gram_new = lax.psum(gram_of(interval_new), "intv")
     day_part = jnp.sum(partial_sums * interval_new[:, None, :], axis=0)

time: 414 us -> 291 us (0.70)
  blocking collectives: 340 us -> 202 us
  waiting for transfers between devices: 0.09 us -> 9.7 us
  starting transfers between devices: 0.08 us -> 6.36 us
    psum x1 -> x0, blocking collectives: 132 us -> none  [body(): interval_sums = lax.psum(interval_part, 'link')]
    ppermute x0 -> x5, waiting for transfers between devices: none -> 9.62 us  [press_threads(): return press_threads(w1 + lax.ppermute(w1, 'link', blocks_here), 2 * y2)]
    psum x1, blocking collectives: 80.1 us -> 72.9 us  [body(): day_sums = lax.psum(day_part, ('link', 'intv'))]
    ppermute x0 -> x5, starting transfers between devices: none -> 6.28 us  [press_threads(): return press_threads(w1 + lax.ppermute(w1, 'link', blocks_here), 2 * y2)]
  transfers between devices with their start and end apart: 2 -> 7, of which waited for: 0 -> 3; matrix products, arithmetic and copies ran while one was open for 6% -> 9% of each run, Pallas kernels for 0% -> 0%
where the time goes in v1:
time: 291 us
  blocking collectives  202 us (69%)
  other arithmetic  38.4 us (13%)
  matrix products  17.7 us (6%)
  between operations  16.3 us (6%)
  waiting for transfers between devices  9.7 us (3%)
  starting transfers between devices  6.36 us (2%)
    psum x1, blocking collectives, body(): gram_link = lax.psum(gram_of(link_new), ('link', 'intv'))  78.3 us
    psum x1, blocking collectives, body(): day_sums = lax.psum(day_part, ('link', 'intv'))  72.9 us
    psum x1, blocking collectives, body(): gram_interval = lax.psum(gram_of(interval_factor), 'intv')  25.9 us
    psum x1, blocking collectives, body(): gram_new = lax.psum(gram_of(interval_new), 'intv')  24.6 us
    another operation x9, other arithmetic, solve_rows(): factor = jnp.linalg.cholesky(shifted)  19.6 us
    another operation x6, other arithmetic, solve_rows(): return jax.scipy.linalg.cho_solve((factor, True), rhs.T).T  16.6 us
    ppermute x5, waiting for transfers between devices, press_threads(): return press_threads(w1 + lax.ppermute(w1, 'link', blocks_here), 2 * y2)  9.62 us
    dot_general x1, matrix products, body(): lax.dot_general(flat, khatri, (((0,), (0,)), ((), ())), preferred_element...  6.38 us
  transfers between devices with their start and end apart: 7, of which 3 were waited for; matrix products, arithmetic and copies ran while one was open for 9% of the time, Pallas kernels for 0%

profile of v1, /device:TPU:32, one launch (start us, length us, event | category | flops | bytes accessed | tf_op | source)
XLA Modules:
  0.0 290.6 jit_solution(6447470152435768004)
XLA Ops:
  7.2 0.0 copy-start.3
  7.2 0.0 copy-start.1
  7.2 0.0 reduce-scatter.2.cloned.1.call-start
  7.2 6.4 %convolution_bitcast_fusion = f32[8192,64]{0,1:T(8,128)} fusion(bf16[32,16,8192]{2,1,0:T(8,128)(2,1)} %param.4, f32[16,64]{1,0:T(8,128)} %param.6, f32[32,64]{1,0:T(8,128)} %param.5), kind=kOutput, calls=%fused_computation | convolution fusion | flops 536936448 | bytes 10498048 | tf_op jit(solution)/shard_map/dot_general | solution.py:31
  13.6 0.0 reduce-scatter.2.cloned.1.call-update
  13.6 0.0 all-gather.2.cloned.1.call-start
  13.7 0.0 copy-done.1
  13.7 0.2 fusion.33
  13.9 25.9 %psum.28 = f32[64,64]{1,0:T(8,128)S(1)} all-reduce(f32[64,64]{1,0:T(8,128)S(1)} %fusion.33), channel_id=1, replica_groups=mesh['link'=32,'intv'=8] {'intv'}, use_global_device_ids=true, to_apply=%region_0.0 | all-reduce | flops 4096 | bytes 32768 | tf_op jit(solution)/shard_map/psum | solution.py:23
  39.8 0.0 copy-done.3
  39.8 0.8 fusion.26
  41.3 0.1 copy.15
  41.4 0.1 copy.16
  41.5 5.9 %cholesky.59 = f32[64,64]{1,0:T(8,128)S(1)} custom-call(f32[64,64]{1,0:T(8,128)S(1)} %copy.16), custom_call_target="Cholesky" | custom-call | tf_op jit(solution)/shard_map/jit(cholesky)/cholesky | solution.py:10
  47.4 0.6 compare_reduce_fusion.2
  48.1 0.7 fusion.2
  48.7 4.9 %custom-call.23 = f32[1,64,64]{1,2,0:T(8,128)S(1)} custom-call(f32[1,64,64]{2,1,0:T(8,128)S(1)} %fusion.2), custom_call_target="InvertDiagBlocksLowerTriangular" | custom-call | tf_op jit(solution)/shard_map/jit(_cho_solve)/triangular_solve | solution.py:11
  53.6 0.0 reduce-scatter.2.cloned.1.call-done
  53.6 1.4 fusion.17
  55.0 0.4 fusion.15
  55.4 0.0 copy-start
  55.4 0.7 bitcast_convert_fusion
  56.1 0.0 all-gather.2.cloned.1.call-update
  56.2 0.4 fusion.34
  56.5 78.3 %psum.29 = f32[64,64]{1,0:T(8,128)S(1)} all-reduce(f32[64,64]{1,0:T(8,128)S(1)} %fusion.34), channel_id=1, replica_groups=mesh['link'=32,'intv'=8] {'link','intv'}, use_global_device_ids=true, to_apply=%region_5.7 | all-reduce | flops 4096 | bytes 32768 | tf_op jit(solution)/shard_map/psum | solution.py:37
  134.8 0.6 fusion.28
  136.1 0.0 all-gather.2.cloned.1.call-done
  136.1 6.4 %convolution_bitcast_fusion.1 = f32[512,64]{0,1:T(8,128)S(1)} fusion(bf16[8192,64]{0,1:T(8,128)(2,1)} %all-gather.2.cloned.1.call-done, bf16[512,8192]{1,0:T(8,128)(2,1)} %bitcast.61), kind=kOutput, calls=%fused_computation.1 | convolution fusion | flops 536870912 | bytes 9568256 | tf_op jit(solution)/shard_map/dot_general | solution.py:39
  142.5 0.1 copy.19
  142.6 0.1 multiply_reduce_fusion.1
  142.7 0.1 collective-permute-start
  142.8 0.1 copy.17
  142.9 3.6 %collective-permute-done = f32[32,64]{1,0:T(8,128)S(1)} collective-permute-done((f32[32,64]{1,0:T(8,128)S(1)}, f32[32,64]{1,0:T(8,128)S(1)}, u32[]{:S(2)}, u32[]{:S(2)}) %collective-permute-start) | collective-permute-done | bytes 8224 | tf_op jit(solution)/shard_map/ppermute | solution.py:53
  146.5 1.2 collective-permute-start.1
  147.8 0.1 copy.18
  147.8 5.9 %cholesky.70 = f32[64,64]{1,0:T(8,128)S(1)} custom-call(f32[64,64]{1,0:T(8,128)S(1)} %copy.18), custom_call_target="Cholesky" | custom-call | tf_op jit(solution)/shard_map/jit(cholesky)/cholesky | solution.py:10
  153.7 0.0 collective-permute-done.1
  153.7 0.8 collective-permute-start.2
  154.6 3.0 %collective-permute-done.2 = f32[32,64]{1,0:T(8,128)S(1)} collective-permute-done((f32[32,64]{1,0:T(8,128)S(1)}, f32[32,64]{1,0:T(8,128)S(1)}, u32[]{:S(2)}, u32[]{:S(2)}) %collective-permute-start.2) | collective-permute-done | bytes 8224 | tf_op jit(solution)/shard_map/ppermute | solution.py:53
  157.5 1.0 collective-permute-start.3
  158.5 0.6 compare_reduce_fusion.1
  159.2 3.0 %collective-permute-done.3 = f32[32,64]{1,0:T(8,128)S(1)} collective-permute-done((f32[32,64]{1,0:T(8,128)S(1)}, f32[32,64]{1,0:T(8,128)S(1)}, u32[]{:S(2)}, u32[]{:S(2)}) %collective-permute-start.3) | collective-permute-done | bytes 8224 | tf_op jit(solution)/shard_map/ppermute | solution.py:53
  162.2 3.1 %collective-permute-start.4 = (f32[32,64]{1,0:T(8,128)S(1)}, f32[32,64]{1,0:T(8,128)S(1)}, u32[]{:S(2)}, u32[]{:S(2)}) collective-permute-start(f32[32,64]{1,0:T(8,128)S(1)} %add.64), channel_id=1, source_target_pairs={{0,128},{8,136},{16,144},{24,152},{32,160},{40,168},{48,176},{56,1... | collective-permute-start | bytes 24584 | tf_op jit(solution)/shard_map/ppermute | solution.py:53
  165.3 0.7 fusion.3
  166.0 4.9 %custom-call.24 = f32[1,64,64]{1,2,0:T(8,128)S(1)} custom-call(f32[1,64,64]{2,1,0:T(8,128)S(1)} %fusion.3), custom_call_target="InvertDiagBlocksLowerTriangular" | custom-call | tf_op jit(solution)/shard_map/jit(_cho_solve)/triangular_solve | solution.py:11
  170.9 0.0 collective-permute-done.4
  170.9 0.2 fusion.12
  171.1 0.2 fusion.10
  171.3 0.0 copy-start.2
  171.4 0.2 fusion.35
  171.6 72.9 %psum.31 = f32[16,64]{1,0:T(8,128)S(1)} all-reduce(f32[16,64]{1,0:T(8,128)S(1)} %multiply_reduce_fusion), channel_id=1, replica_groups=mesh['link'=32,'intv'=8] {'link','intv'}, use_global_device_ids=true, to_apply=%region_11.13 | all-reduce | flops 1024 | bytes 8192 | tf_op jit(solution)/shard_map/psum | solution.py:61
  244.5 24.6 %psum.30 = f32[64,64]{1,0:T(8,128)S(1)} all-reduce(f32[64,64]{1,0:T(8,128)S(1)} %fusion.35), channel_id=1, replica_groups=mesh['link'=32,'intv'=8] {'intv'}, use_global_device_ids=true, to_apply=%region_8.10 | all-reduce | flops 4096 | bytes 32768 | tf_op jit(solution)/shard_map/psum | solution.py:59
  269.1 0.6 fusion.30
  270.4 0.1 copy.20
  270.5 0.1 copy.21
  270.5 5.9 %cholesky.81 = f32[64,64]{1,0:T(8,128)S(1)} custom-call(f32[64,64]{1,0:T(8,128)S(1)} %copy.21), custom_call_target="Cholesky" | custom-call | tf_op jit(solution)/shard_map/jit(cholesky)/cholesky | solution.py:10
  276.4 0.6 compare_reduce_fusion
  277.1 0.7 fusion.4
  277.7 4.9 %custom-call.25 = f32[1,64,64]{1,2,0:T(8,128)S(1)} custom-call(f32[1,64,64]{2,1,0:T(8,128)S(1)} %fusion.4), custom_call_target="InvertDiagBlocksLowerTriangular" | custom-call | tf_op jit(solution)/shard_map/jit(_cho_solve)/triangular_solve | solution.py:11
  282.6 0.3 fusion.7
  282.9 0.8 fusion.5
  283.7 0.0 copy-done
  283.7 0.0 copy-done.2
  (14 shorter events, 0.2 us)
Async XLA Ops:
  7.2 32.7 %copy-start.3 = (f32[16,64]{1,0:T(8,128)S(1)}, f32[16,64]{1,0:T(8,128)}, u32[]{:S(2)}) copy-start(f32[16,64]{1,0:T(8,128)} %param.6) | copy-start | bytes 12292
  7.2 6.5 %copy-start.1 = (f32[32,64]{1,0:T(8,128)S(1)}, f32[32,64]{1,0:T(8,128)}, u32[]{:S(2)}) copy-start(f32[32,64]{1,0:T(8,128)} %param.5) | copy-start | bytes 24580
  7.2 46.4 %reduce-scatter.2.cloned.1.call-start = ((), (), s32[]{:S(2)}) async-start(), calls=%async_computation.1 | async-start | bytes 2359296 | tf_op jit(solution)/shard_map/reduce_scatter | solution.py:30
  13.6 122.4 %all-gather.2.cloned.1.call-start = ((), (), s32[]{:S(2)}) async-start(), calls=%async_computation.2 | async-start | bytes 1179648 | tf_op jit(solution)/shard_map/all_gather | solution.py:38
  55.4 228.4 %copy-start = (f32[64,1024]{1,0:T(8,128)}, f32[64,1024]{1,0:T(8,128)S(1)}, u32[]{:S(2)}) copy-start(f32[64,1024]{1,0:T(8,128)S(1)} %fusion.15) | copy-start | bytes 786436
  142.7 3.8 %collective-permute-start = (f32[32,64]{1,0:T(8,128)S(1)}, f32[32,64]{1,0:T(8,128)S(1)}, u32[]{:S(2)}, u32[]{:S(2)}) collective-permute-start(f32[32,64]{1,0:T(8,128)S(1)} %multiply_reduce_fusion.1), channel_id=1, source_target_pairs={{0,8},{8,0},{16,24},{24,16},{32,40},{40,32},{48,56},{56,48},{64,72... | collective-permute-start | bytes 24584 | tf_op jit(solution)/shard_map/ppermute | solution.py:53
  146.5 7.2 %collective-permute-start.1 = (f32[32,64]{1,0:T(8,128)S(1)}, f32[32,64]{1,0:T(8,128)S(1)}, u32[]{:S(2)}, u32[]{:S(2)}) collective-permute-start(f32[32,64]{1,0:T(8,128)S(1)} %add.61), channel_id=1, source_target_pairs={{0,16},{8,24},{16,0},{24,8},{32,48},{40,56},{48,32},{56,40},{64,80... | collective-permute-start | bytes 24584 | tf_op jit(solution)/shard_map/ppermute | solution.py:53
  153.7 3.8 %collective-permute-start.2 = (f32[32,64]{1,0:T(8,128)S(1)}, f32[32,64]{1,0:T(8,128)S(1)}, u32[]{:S(2)}, u32[]{:S(2)}) collective-permute-start(f32[32,64]{1,0:T(8,128)S(1)} %add.62), channel_id=1, source_target_pairs={{0,32},{8,40},{16,48},{24,56},{32,0},{40,8},{48,16},{56,24},{64,96... | collective-permute-start | bytes 24584 | tf_op jit(solution)/shard_map/ppermute | solution.py:53
  157.5 4.6 %collective-permute-start.3 = (f32[32,64]{1,0:T(8,128)S(1)}, f32[32,64]{1,0:T(8,128)S(1)}, u32[]{:S(2)}, u32[]{:S(2)}) collective-permute-start(f32[32,64]{1,0:T(8,128)S(1)} %add.63), channel_id=1, source_target_pairs={{0,64},{8,72},{16,80},{24,88},{32,96},{40,104},{48,112},{56,120},{... | collective-permute-start | bytes 24584 | tf_op jit(solution)/shard_map/ppermute | solution.py:53
  162.2 8.7 %collective-permute-start.4 = (f32[32,64]{1,0:T(8,128)S(1)}, f32[32,64]{1,0:T(8,128)S(1)}, u32[]{:S(2)}, u32[]{:S(2)}) collective-permute-start(f32[32,64]{1,0:T(8,128)S(1)} %add.64), channel_id=1, source_target_pairs={{0,128},{8,136},{16,144},{24,152},{32,160},{40,168},{48,176},{56,1... | collective-permute-start | bytes 24584 | tf_op jit(solution)/shard_map/ppermute | solution.py:53
  171.3 112.4 %copy-start.2 = (f32[64,32]{0,1:T(8,128)}, f32[64,32]{0,1:T(8,128)S(1)}, u32[]{:S(2)}) copy-start(f32[64,32]{0,1:T(8,128)S(1)} %fusion.10) | copy-start | bytes 24580
Sparse Core Ops, SparseCore 0:
  13.8 38.9 reduce-scatter.1
  56.3 25.9 all-gather.1
